TPU v7x, 512 devices: a whole 4x4x16 slice. The times are simulated.
512 devices in a mesh: ctx: 128 (over z, y_lo, x), ch: 4 (over y_hi, core).
Axes of the slice: x: 4, y: 4 (y_hi: 2, y_lo: 2; y = y_hi * 2 + y_lo), z: 16, core: 2. Of those that a mesh axis runs over, the one named last changes fastest.
Arguments:
- tokens: bfloat16 [16384, 4096], P('ctx'), may hold values from -1000 to 1000, as said below
- norm_gain: float32 [4096], replicated, may hold values from 0.1 to 1.9
- in_proj: bfloat16 [4096, 3, 2048], P('ctx', None, 'ch'), may hold values from -0.09375 to 0.09375
- short_taps: float32 [3, 3, 2048], P(None, None, 'ch'), may hold values from -3 to 3
- decay: float32 [16, 2048], P(None, 'ch'), may hold values from 0 to 1, as said below
- residue: float32 [16, 2048], P(None, 'ch'), may hold values from -1.5 to 1.5
- skip: float32 [2048], P('ch'), may hold values from -4 to 4
Outputs:
- mixed: bfloat16 [16384, 2048], P('ctx', 'ch')
Inputs may be any that keep to these rules, and one draw needn't show every extreme that they name: `tokens`: every entry is finite. `decay`: every rate is positive.
All inputs are finite; a program needn't handle non-finite values.
Results may differ from a plain program's by a relative error of at most 0.01295.
Values may be sent and summed in bfloat16 or wider, within the bound.
A program may use at most 128 MiB of HBM per device.

v0:
```python
import math
import jax
import jax.numpy as jnp
from jax import lax
from jax.sharding import PartitionSpec as P


def passed_along(value, axis, steps):
    count = lax.axis_size(axis)
    initial, last = (max(0, -steps), min(count, count - steps))
    return lax.ppermute(value, axis, [(source, source + steps) for source in range(initial, last)])


def shortened(array):
    return jax.tree.map(lambda a: a.astype(jnp.bfloat16) if a.dtype == jnp.float32 else a, array)


def phase_table(left_index, right_index, period):
    product = left_index[:, None] * right_index[None, :] % period
    product = jnp.where(product > period // 2, product - period, product)
    return product.astype(jnp.float32) * (2.0 * math.pi / period)


def contract_rows(matrix, values):
    return jnp.einsum("sr,krc->ksc", matrix, values, precision=lax.Precision.HIGHEST)


def first_forward(blocks, r_index, total_len):
    count = blocks.shape[0]
    freq_index = jnp.arange(2 * count, dtype=jnp.int32)
    phases = phase_table(freq_index, jnp.arange(count, dtype=jnp.int32), 2 * count)
    flat = blocks.reshape(count, -1)
    out_shape = (2 * count,) + blocks.shape[1:]
    real_part = jnp.dot(jnp.cos(phases), flat, precision=lax.Precision.HIGHEST).reshape(out_shape)
    imag_part = -jnp.dot(jnp.sin(phases), flat, precision=lax.Precision.HIGHEST).reshape(out_shape)
    twist = phase_table(freq_index, r_index, total_len)
    cosine = jnp.cos(twist)[:, :, None]
    sine = jnp.sin(twist)[:, :, None]
    return (real_part * cosine + imag_part * sine, imag_part * cosine - real_part * sine)


def second_forward(real_part, imag_part):
    length = real_part.shape[1]
    steps_index = jnp.arange(length, dtype=jnp.int32)
    phases = phase_table(steps_index, steps_index, length)
    cosine = jnp.cos(phases)
    sine = jnp.sin(phases)
    out_real = contract_rows(cosine, real_part) + contract_rows(sine, imag_part)
    out_imag = contract_rows(cosine, imag_part) - contract_rows(sine, real_part)
    return (out_real, out_imag)


def first_inverse(real_part, imag_part, freq_index, total_len):
    length = real_part.shape[1]
    steps_index = jnp.arange(length, dtype=jnp.int32)
    phases = phase_table(steps_index, steps_index, length)
    cosine = jnp.cos(phases)
    sine = jnp.sin(phases)
    mid_real = contract_rows(cosine, real_part) - contract_rows(sine, imag_part)
    mid_imag = contract_rows(cosine, imag_part) + contract_rows(sine, real_part)
    twist = phase_table(freq_index, steps_index, total_len)
    tw_cos = jnp.cos(twist)[:, :, None]
    tw_sin = jnp.sin(twist)[:, :, None]
    return (mid_real * tw_cos - mid_imag * tw_sin, mid_imag * tw_cos + mid_real * tw_sin)


def second_inverse(real_part, imag_part, total_len):
    doubled = real_part.shape[0]
    count = doubled // 2
    phases = phase_table(
        jnp.arange(count, dtype=jnp.int32), jnp.arange(doubled, dtype=jnp.int32), doubled
    )
    flat_real = real_part.reshape(doubled, -1)
    flat_imag = imag_part.reshape(doubled, -1)
    result = jnp.dot(jnp.cos(phases), flat_real, precision=lax.Precision.HIGHEST)
    result = result - jnp.dot(jnp.sin(phases), flat_imag, precision=lax.Precision.HIGHEST)
    return (result * (1.0 / total_len)).reshape((count,) + real_part.shape[1:])


def spectrum(freq_index, decay_cols, residue_cols, length, count, seq_len, total_len):
    freq = freq_index[:, None] + 2 * count * jnp.arange(length, dtype=jnp.int32)[None, :]
    symmetric = jnp.where(freq > total_len // 2, freq - total_len, freq)
    half_phase = symmetric.astype(jnp.float32) * (math.pi / total_len)
    half_sq = (jnp.sin(half_phase) ** 2)[:, :, None]
    full_sin = jnp.sin(2.0 * half_phase)[:, :, None]
    parity = (1 - 2 * (freq % 2)).astype(jnp.float32)[:, :, None]
    shape_out = (freq_index.shape[0], length, decay_cols.shape[1])

    def add_mode(mode, carried):
        acc_real, acc_imag = carried
        rate = decay_cols[mode]
        amplitude = residue_cols[mode] * jnp.sqrt(2.0 * rate)
        ratio = jnp.exp(-rate)
        gap_term = -jnp.expm1(-rate)
        tail_term = jnp.exp(-rate * seq_len)
        along = gap_term + 2.0 * ratio * half_sq
        across = ratio * full_sin
        denom = gap_term * gap_term + 4.0 * ratio * half_sq
        numer = amplitude * (1.0 - tail_term * parity) / denom
        return (acc_real + numer * along, acc_imag - numer * across)

    zeros_block = jnp.zeros(shape_out, jnp.float32)
    return lax.fori_loop(0, decay_cols.shape[0], add_mode, (zeros_block, zeros_block))


def local(tokens, norm_gain, in_proj, short_taps, decay, residue, skip):
    tok_rows = tokens.shape[0]
    channels = in_proj.shape[2]
    devices = lax.axis_size("ctx")
    position = lax.axis_index("ctx")
    as_float = tokens.astype(jnp.float32)
    mean_square = jnp.mean(as_float * as_float, axis=1, keepdims=True)
    normed = (as_float * lax.rsqrt(mean_square + 1e-06) * norm_gain).astype(jnp.bfloat16)
    weight_piece = lax.all_gather(in_proj, "ctx", axis=0, tiled=True)
    piece_rows = weight_piece.shape[0]
    flat_piece = weight_piece.reshape(piece_rows, 3 * channels)
    projected = jnp.dot(normed, flat_piece, preferred_element_type=jnp.float32)
    proj = projected.astype(jnp.bfloat16).reshape(tok_rows, 3, channels)
    tap_count = short_taps.shape[0]
    rim_rows = passed_along(proj[tok_rows - (tap_count - 1) :], "ctx", 1)
    extended = jnp.concatenate([rim_rows, proj], axis=0)
    feats = jnp.zeros((tok_rows, 3, channels), jnp.float32)
    for shift_by in range(tap_count):
        window = extended[tap_count - 1 - shift_by : tap_count - 1 - shift_by + tok_rows].astype(
            jnp.float32
        )
        feats = feats + short_taps[shift_by] * window
    drive = feats[:, 1, :] * feats[:, 2, :]
    seq_len = tok_rows * devices
    total_len = 2 * seq_len
    group_rows = tok_rows // devices
    regrouped = drive.reshape(devices, group_rows, channels)
    arrived = lax.all_to_all(
        regrouped.astype(jnp.bfloat16), "ctx", split_axis=0, concat_axis=0, tiled=True
    ).astype(regrouped.dtype)
    r_index = position * group_rows + jnp.arange(group_rows, dtype=jnp.int32)
    front_real, front_imag = first_forward(arrived, r_index, total_len)
    middle = lax.all_to_all(
        jnp.stack([front_real, front_imag]).astype(jnp.bfloat16),
        "ctx",
        split_axis=1,
        concat_axis=2,
        tiled=True,
    ).astype(jnp.float32)
    spec_real, spec_imag = second_forward(middle[0], middle[1])
    freq_index = 2 * position + jnp.arange(2, dtype=jnp.int32)
    filt_real, filt_imag = spectrum(
        freq_index, decay, residue, tok_rows, devices, seq_len, total_len
    )
    prod_real = spec_real * filt_real - spec_imag * filt_imag
    prod_imag = spec_real * filt_imag + spec_imag * filt_real
    back_real, back_imag = first_inverse(prod_real, prod_imag, freq_index, total_len)
    returned = lax.all_to_all(
        shortened(jnp.stack([back_real, back_imag])), "ctx", split_axis=2, concat_axis=1, tiled=True
    )
    local_conv = second_inverse(returned[0], returned[1], total_len)
    conv = (
        lax.all_to_all(shortened(local_conv), "ctx", split_axis=0, concat_axis=1, tiled=True)
        .astype(local_conv.dtype)
        .reshape(tok_rows, channels)
    )
    return (feats[:, 0, :] * (conv + skip * drive)).astype(jnp.bfloat16)


def solution(mesh):
    placed = (
        P("ctx", None),
        P(),
        P("ctx", None, "ch"),
        P(None, None, "ch"),
        P(None, "ch"),
        P(None, "ch"),
        P("ch"),
    )
    return jax.shard_map(
        local, mesh=mesh, in_specs=placed, out_specs=P("ctx", "ch"), check_vma=False
    )
```

profile of v0, /device:TPU:8, one launch (start us, length us, event | category | flops | bytes accessed | tf_op | source)
XLA Modules:
  0.0 810.4 jit_solution(1913601212873430210)
XLA Ops:
  6.5 0.7 all-gather.2.cloned.1.call-update
  7.3 1.5 fusion.13
  8.8 611.6 %all-gather.2.cloned.1.call-done = bf16[4096,3,512]{2,0,1:T(8,128)(2,1)} async-done(((bf16[32,3,512]{2,0,1:T(8,128)(2,1)}), bf16[4096,3,512]{2,0,1:T(8,128)(2,1)}) %all-gather.2.cloned.1.call-update) | async-done | bytes 12582928 | tf_op jit(solution)/shard_map/all_gather | solution.py:114
  620.4 17.0 %copy.55 = bf16[4096,3,512]{0,2,1:T(8,128)(2,1)} copy(bf16[4096,3,512]{2,0,1:T(8,128)(2,1)} %all-gather.2.cloned.1.call-done) | data formatting | bytes 25165824 | tf_op jit(solution)/shard_map/all_gather | solution.py:114
  637.4 8.9 %convolution_convert_fusion = bf16[128,1536]{1,0:T(8,128)(2,1)S(1)} fusion(bf16[4096,1536]{0,1:T(8,128)(2,1)} %bitcast.120, bf16[128,4096]{1,0:T(8,128)(2,1)S(1)} %copy-done, f32[4096]{0:T(1024)S(1)} %copy-done.2, f32[128]{0:T(128)S(1)} %add_rsqrt_fusion), kind=kOutput, calls=%fused_computation.30 | convolution fusion | flops 1612906496 | bytes 14041600 | tf_op jit(solution)/shard_map/dot_general | solution.py:117
  646.6 3.3 collective-permute-start
  650.2 10.0 %collective-permute-done = bf16[2,3,512]{0,2,1:T(8,128)(2,1)S(1)} collective-permute-done((bf16[2,3,512]{0,2,1:T(8,128)(2,1)S(1)}, bf16[2,3,512]{0,2,1:T(8,128)(2,1)S(1)}, u32[]{:S(2)}, u32[]{:S(2)}) %collective-permute-start) | collective-permute-done | bytes 6176 | tf_op jit(solution)/shard_map/ppermute | solution.py:11
  660.2 1.1 multiply_add_fusion
  661.3 0.6 broadcast.788
  661.9 0.7 reduce
  662.6 0.7 reshape.468
  663.3 16.9 %all-to-all-start = ((bf16[128,2,256]{2,1,0:T(2,128)(2,1)}), bf16[128,2,256]{2,1,0:T(2,128)(2,1)S(1)}, u32[]{:S(2)}, u32[]{:S(2)}) async-start(bf16[128,2,256]{2,1,0:T(2,128)(2,1)} %reshape.468), calls=%async_computation | async-start | bytes 262144 | tf_op jit(solution)/shard_map/all_to_all | solution.py:133
  680.3 16.6 %all-to-all-done = bf16[128,2,256]{2,1,0:T(2,128)(2,1)S(1)} async-done(((bf16[128,2,256]{2,1,0:T(2,128)(2,1)}), bf16[128,2,256]{2,1,0:T(2,128)(2,1)S(1)}, u32[]{:S(2)}, u32[]{:S(2)}) %all-to-all-start) | async-done | bytes 131104 | tf_op jit(solution)/shard_map/all_to_all | solution.py:133
  697.0 0.8 convolution_negate_fusion
  697.9 0.9 fusion.25
  698.8 1.3 copy.59
  700.2 5.8 all-to-all-start.1
  705.9 22.7 %while.18 = (s32[]{:T(128)}, f32[2,128,512]{2,1,0:T(8,128)S(1)}, f32[2,128,512]{2,1,0:T(8,128)S(1)}, f32[16,512]{1,0:T(8,128)}, f32[16,512]{1,0:T(8,128)}, /*ind...) while((s32[]{:T(128)}, f32[2,128,512]{2,1,0:T(8,128)S(1)}, ...), condition=%wide.region_2.3_spmd.clone.clone.clone, body=%wide.region_1.2_spmd.clone.clone.clone.sunk | while | flops 1976067 | bytes 2139267 | solution.py:103
  706.1 0.8 sqrt_multiply_fusion.2
  706.9 0.4 select_subtract_fusion.2
  707.5 0.8 sqrt_multiply_fusion.2
  708.3 0.4 select_subtract_fusion.2
  708.9 0.8 sqrt_multiply_fusion.2
  709.8 0.4 select_subtract_fusion.2
  710.3 0.8 sqrt_multiply_fusion.2
  711.2 0.4 select_subtract_fusion.2
  711.7 0.8 sqrt_multiply_fusion.2
  712.6 0.4 select_subtract_fusion.2
  713.2 0.8 sqrt_multiply_fusion.2
  714.0 0.4 select_subtract_fusion.2
  714.6 0.8 sqrt_multiply_fusion.2
  715.4 0.4 select_subtract_fusion.2
  716.0 0.8 sqrt_multiply_fusion.2
  716.9 0.4 select_subtract_fusion.2
  717.4 0.8 sqrt_multiply_fusion.2
  718.3 0.4 select_subtract_fusion.2
  718.8 0.8 sqrt_multiply_fusion.2
  719.7 0.4 select_subtract_fusion.2
  720.3 0.8 sqrt_multiply_fusion.2
  721.1 0.4 select_subtract_fusion.2
  721.7 0.8 sqrt_multiply_fusion.2
  722.5 0.4 select_subtract_fusion.2
  723.1 0.8 sqrt_multiply_fusion.2
  724.0 0.4 select_subtract_fusion.2
  724.5 0.8 sqrt_multiply_fusion.2
  725.4 0.4 select_subtract_fusion.2
  725.9 0.8 sqrt_multiply_fusion.2
  727.4 0.8 sqrt_multiply_fusion.2
  729.5 0.5 copy.60
  730.1 0.6 fusion.31
  730.7 0.6 fusion.32
  731.3 0.6 fusion.17
  732.0 0.7 multiply_add_fusion.1
  732.7 0.8 fusion.61
  733.5 0.8 fusion.63
  734.3 0.8 convolution_add_fusion
  735.2 0.9 fusion.27
  736.2 0.5 copy.65
  736.7 40.1 %all_to_all.44 = bf16[2,2,128,512]{3,1,0,2:T(2,128)(2,1)S(1)} all-to-all(bf16[2,2,128,512]{3,1,0,2:T(2,128)(2,1)S(1)} %copy.65), channel_id=1, replica_groups=mesh['ctx'=128,'ch'=4] {'ctx'}, dimensions={2} | all-to-all | bytes 1048576 | tf_op jit(solution)/shard_map/all_to_all | solution.py:153
  777.3 0.8 fusion.47
  778.2 0.8 fusion.20
  779.0 0.7 reduce.1
  779.7 22.6 %all_to_all.45 = bf16[128,2,256]{2,1,0:T(2,128)(2,1)S(1)} all-to-all(bf16[128,2,256]{2,1,0:T(2,128)(2,1)S(1)} %reshape.470), channel_id=1, replica_groups=mesh['ctx'=128,'ch'=4] {'ctx'}, dimensions={0} | all-to-all | bytes 262144 | tf_op jit(solution)/shard_map/all_to_all | solution.py:158
  802.7 0.8 copy.68
  (85 shorter events, 7.0 us)
Async XLA Ops:
  6.5 613.9 %all-gather.2.cloned.1.call-start = ((), (), s32[]{:S(2)}) async-start(), calls=%async_computation.4 | async-start | bytes 12681216 | tf_op jit(solution)/shard_map/all_gather | solution.py:114
  8.8 628.6 %copy-start = (bf16[128,4096]{1,0:T(8,128)(2,1)S(1)}, bf16[128,4096]{1,0:T(8,128)(2,1)}, u32[]{:S(2)}) copy-start(bf16[128,4096]{1,0:T(8,128)(2,1)} %param.9) | copy-start | bytes 3145732
  8.8 628.6 %copy-start.2 = (f32[4096]{0:T(1024)S(1)}, f32[4096]{0:T(1024)}, u32[]{:S(2)}) copy-start(f32[4096]{0:T(1024)} %param.10) | copy-start | bytes 49156
  637.4 12.5 %copy-start.1 = (f32[3,3,512]{2,1,0:T(4,128)S(1)}, f32[3,3,512]{2,1,0:T(4,128)}, u32[]{:S(2)}) copy-start(f32[3,3,512]{2,1,0:T(4,128)} %param.12) | copy-start | bytes 55300
  646.6 13.6 %collective-permute-start = (bf16[2,3,512]{0,2,1:T(8,128)(2,1)S(1)}, bf16[2,3,512]{0,2,1:T(8,128)(2,1)S(1)}, u32[]{:S(2)}, u32[]{:S(2)}) collective-permute-start(bf16[2,3,512]{0,2,1:T(8,128)(2,1)S(1)} %bitcast.130), channel_id=1, source_target_pairs={{0,4},{4,8},{8,12},{12,16},{16,20},{20,24},{24,28},{28,32},{32,36}... | collective-permute-start | bytes 18440 | tf_op jit(solution)/shard_map/ppermute | solution.py:11
  663.3 33.6 %all-to-all-start = ((bf16[128,2,256]{2,1,0:T(2,128)(2,1)}), bf16[128,2,256]{2,1,0:T(2,128)(2,1)S(1)}, u32[]{:S(2)}, u32[]{:S(2)}) async-start(bf16[128,2,256]{2,1,0:T(2,128)(2,1)} %reshape.468), calls=%async_computation | async-start | bytes 262144 | tf_op jit(solution)/shard_map/all_to_all | solution.py:133
  700.2 29.4 %all-to-all-start.1 = ((bf16[2,256,1,512]{3,0,2,1:T(2,128)(2,1)}), bf16[2,256,1,512]{3,0,2,1:T(2,128)(2,1)S(1)}, u32[]{:S(2)}, u32[]{:S(2)}) async-start(bf16[2,256,1,512]{3,0,2,1:T(2,128)(2,1)} %copy.59), calls=%async_computation.1 | async-start | bytes 1048576 | tf_op jit(solution)/shard_map/all_to_all | solution.py:138
  777.2 25.4 %copy-start.3 = (f32[512]{0:T(512)S(1)}, f32[512]{0:T(512)}, u32[]{:S(2)}) copy-start(f32[512]{0:T(512)} %param.15) | copy-start | bytes 6148
Sparse Core Ops, SparseCore 0:
  9.4 610.8 all-gather.1
where the time goes:
time: 814 us; the launch traced here: 810 us
  waiting for transfers between devices  639 us (79%)
  blocking collectives  62.8 us (8%)
  other arithmetic  26.5 us (3%)
  starting transfers between devices  26 us (3%)
  local copies, waits for them, and re-layouts  23.4 us (3%)
  matrix products  18.1 us (2%)
  between operations  13.7 us (2%)
    all_gather x1, waiting for transfers between devices, local(): weight_piece = lax.all_gather(in_proj, 'ctx', axis=0, tiled=True)  612 us
    all_to_all x1, blocking collectives, local(): lax.all_to_all(shortened(jnp.stack([back_real, back_imag])), 'ctx', split...  40.1 us
    all_to_all x1, blocking collectives, local(): lax.all_to_all(shortened(local_conv), 'ctx', split_axis=0, concat_axis=1,...  22.6 us
    all_gather x1, local copies, waits for them, and re-layouts, local(): weight_piece = lax.all_gather(in_proj, 'ctx', axis=0, tiled=True)  17 us
    all_to_all x1, starting transfers between devices, local(): lax.all_to_all(regrouped.astype(jnp.bfloat16), 'ctx', split_axis=0, conca...  16.9 us
    all_to_all x1, waiting for transfers between devices, local(): lax.all_to_all(regrouped.astype(jnp.bfloat16), 'ctx', split_axis=0, conca...  16.6 us
  transfers between devices with their start and end apart: 4, of which 4 were waited for; matrix products, arithmetic and copies ran while one was open for 3% of the time, Pallas kernels for 0%

commit v1 on v0

--- a/solution.py
+++ b/solution.py
@@ -111,7 +111,9 @@
     as_float = tokens.astype(jnp.float32)
     mean_square = jnp.mean(as_float * as_float, axis=1, keepdims=True)
     normed = (as_float * lax.rsqrt(mean_square + 1e-06) * norm_gain).astype(jnp.bfloat16)
-    weight_piece = lax.all_gather(in_proj, "ctx", axis=0, tiled=True)
+    weight_piece = jnp.concatenate(
+        lax.all_to_all(jnp.stack([in_proj] * lax.axis_size("ctx")), "ctx", 0, 0), axis=0
+    )
     piece_rows = weight_piece.shape[0]
     flat_piece = weight_piece.reshape(piece_rows, 3 * channels)
     projected = jnp.dot(normed, flat_piece, preferred_element_type=jnp.float32)

time: 814 us -> 764 us (0.939)
  the two profiles are of different devices: /device:TPU:8 before, /device:TPU:24 now
where the time goes in v1:
time: 764 us; the launch traced here: 761 us
  waiting for transfers between devices  580 us (76%)
  blocking collectives  62.1 us (8%)
  starting transfers between devices  43.4 us (6%)
  local copies, waits for them, and re-layouts  37.7 us (5%)
  other arithmetic  25.1 us (3%)
  matrix products  11.2 us (1%)
    all_to_all x1, waiting for transfers between devices, local(): lax.all_to_all(jnp.stack([in_proj] * lax.axis_size('ctx')), 'ctx', 0, 0)  545 us
    all_to_all x1, blocking collectives, local(): lax.all_to_all(shortened(jnp.stack([back_real, back_imag])), 'ctx', split...  39.5 us
    all_to_all x1, blocking collectives, local(): lax.all_to_all(shortened(local_conv), 'ctx', split_axis=0, concat_axis=1,...  22.6 us
    all_to_all x1, starting transfers between devices, local(): lax.all_to_all(jnp.stack([in_proj] * lax.axis_size('ctx')), 'ctx', 0, 0)  20.9 us
    all_to_all x1, waiting for transfers between devices, local(): lax.all_to_all(regrouped.astype(jnp.bfloat16), 'ctx', split_axis=0, conca...  16.8 us
    all_to_all x1, local copies, waits for them, and re-layouts, local(): lax.all_to_all(jnp.stack([in_proj] * lax.axis_size('ctx')), 'ctx', 0, 0)  16.7 us
  transfers between devices with their start and end apart: 4, of which 4 were waited for; matrix products, arithmetic and copies ran while one was open for 3% of the time, Pallas kernels for 0%

profile of v1, /device:TPU:24, one launch (start us, length us, event | category | flops | bytes accessed | tf_op | source)
XLA Modules:
  0.0 760.7 jit_solution(9026255348213398489)
XLA Ops:
  0.0 7.0 stack.17
  7.0 20.9 %all-to-all-start = ((bf16[128,32,3,512]{3,1,2,0:T(8,128)(2,1)}), bf16[128,32,3,512]{3,1,2,0:T(8,128)(2,1)}, u32[]{:S(2)}, u32[]{:S(2)}) async-start(bf16[128,32,3,512]{3,1,2,0:T(8,128)(2,1)} %stack.17), calls=%async_computation | async-start | bytes 25165824 | tf_op jit(solution)/shard_map/all_to_all | solution.py:115
  28.2 544.8 %all-to-all-done = bf16[128,32,3,512]{3,1,2,0:T(8,128)(2,1)} async-done(((bf16[128,32,3,512]{3,1,2,0:T(8,128)(2,1)}), bf16[128,32,3,512]{3,1,2,0:T(8,128)(2,1)}, u32[]{:S(2)}, u32[]{:S(2)}) %all-to-all-start) | async-done | bytes 12582944 | tf_op jit(solution)/shard_map/all_to_all | solution.py:115
  573.0 16.7 %copy.56 = bf16[128,32,3,512]{3,2,1,0:T(4,128)(2,1)S(1)} copy(bf16[128,32,3,512]{3,1,2,0:T(8,128)(2,1)} %all-to-all-done) | data formatting | bytes 25165824 | tf_op jit(solution)/shard_map/all_to_all | solution.py:115
  589.8 7.6 %copy.72 = bf16[512,8,3,512]{3,1,2,0:T(8,128)(2,1)S(1)} copy(bf16[512,8,3,512]{3,2,1,0:T(4,128)(2,1)S(1)} %bitcast.123) | data formatting | bytes 25165824
  597.4 2.0 convolution_convert_fusion
  599.7 2.4 collective-permute-start
  602.4 9.1 %collective-permute-done = bf16[2,3,512]{0,2,1:T(8,128)(2,1)S(1)} collective-permute-done((bf16[2,3,512]{0,2,1:T(8,128)(2,1)S(1)}, bf16[2,3,512]{0,2,1:T(8,128)(2,1)S(1)}, u32[]{:S(2)}, u32[]{:S(2)}) %collective-permute-start) | collective-permute-done | bytes 6176 | tf_op jit(solution)/shard_map/ppermute | solution.py:11
  611.5 1.1 multiply_add_fusion
  612.6 0.5 broadcast.790
  613.1 0.6 reduce
  613.8 0.7 reshape.466
  614.5 14.1 %all-to-all-start.1 = ((bf16[128,2,256]{2,1,0:T(2,128)(2,1)}), bf16[128,2,256]{2,1,0:T(2,128)(2,1)S(1)}, u32[]{:S(2)}, u32[]{:S(2)}) async-start(bf16[128,2,256]{2,1,0:T(2,128)(2,1)} %reshape.466), calls=%async_computation.1 | async-start | bytes 262144 | tf_op jit(solution)/shard_map/all_to_all | solution.py:135
  628.7 16.8 %all-to-all-done.1 = bf16[128,2,256]{2,1,0:T(2,128)(2,1)S(1)} async-done(((bf16[128,2,256]{2,1,0:T(2,128)(2,1)}), bf16[128,2,256]{2,1,0:T(2,128)(2,1)S(1)}, u32[]{:S(2)}, u32[]{:S(2)}) %all-to-all-start.1) | async-done | bytes 131104 | tf_op jit(solution)/shard_map/all_to_all | solution.py:135
  645.6 0.8 convolution_negate_fusion
  646.4 0.9 fusion.25
  647.4 1.3 copy.60
  648.7 6.0 all-to-all-start.2
  654.7 22.7 %while.18 = (s32[]{:T(128)}, f32[2,128,512]{2,1,0:T(8,128)S(1)}, f32[2,128,512]{2,1,0:T(8,128)S(1)}, f32[16,512]{1,0:T(8,128)}, f32[16,512]{1,0:T(8,128)}, /*ind...) while((s32[]{:T(128)}, f32[2,128,512]{2,1,0:T(8,128)S(1)}, ...), condition=%wide.region_2.3_spmd.clone.clone.clone, body=%wide.region_1.2_spmd.clone.clone.clone.sunk | while | flops 1976067 | bytes 2139267 | solution.py:103
  654.8 0.8 sqrt_multiply_fusion.2
  655.7 0.4 select_subtract_fusion.2
  656.3 0.8 sqrt_multiply_fusion.2
  657.1 0.4 select_subtract_fusion.2
  657.7 0.8 sqrt_multiply_fusion.2
  658.5 0.4 select_subtract_fusion.2
  659.1 0.8 sqrt_multiply_fusion.2
  660.0 0.4 select_subtract_fusion.2
  660.5 0.8 sqrt_multiply_fusion.2
  661.4 0.4 select_subtract_fusion.2
  661.9 0.8 sqrt_multiply_fusion.2
  662.8 0.4 select_subtract_fusion.2
  663.4 0.8 sqrt_multiply_fusion.2
  664.2 0.4 select_subtract_fusion.2
  664.8 0.8 sqrt_multiply_fusion.2
  665.6 0.4 select_subtract_fusion.2
  666.2 0.8 sqrt_multiply_fusion.2
  667.1 0.4 select_subtract_fusion.2
  667.6 0.8 sqrt_multiply_fusion.2
  668.5 0.4 select_subtract_fusion.2
  669.0 0.8 sqrt_multiply_fusion.2
  669.9 0.4 select_subtract_fusion.2
  670.5 0.8 sqrt_multiply_fusion.2
  671.3 0.4 select_subtract_fusion.2
  671.9 0.8 sqrt_multiply_fusion.2
  673.3 0.8 sqrt_multiply_fusion.2
  674.7 0.8 sqrt_multiply_fusion.2
  676.1 0.8 sqrt_multiply_fusion.2
  678.0 9.5 %all-to-all-done.2 = bf16[2,256,1,512]{3,0,2,1:T(2,128)(2,1)S(1)} async-done(((bf16[2,256,1,512]{3,0,2,1:T(2,128)(2,1)}), bf16[2,256,1,512]{3,0,2,1:T(2,128)(2,1)S(1)}, u32[]{:S(2)}, u32[]{:S(2)}) %all-to-all-start.2) | async-done | bytes 524320 | tf_op jit(solution)/shard_map/all_to_all | solution.py:140
  687.5 0.5 copy.61
  688.0 0.6 fusion.31
  688.7 0.6 fusion.32
  689.3 0.6 fusion.17
  689.9 0.7 multiply_add_fusion.1
  690.6 0.8 fusion.61
  691.5 0.8 fusion.63
  692.3 0.8 convolution_add_fusion
  693.1 0.9 fusion.27
  694.1 0.5 copy.66
  694.6 39.5 %all_to_all.49 = bf16[2,2,128,512]{3,1,0,2:T(2,128)(2,1)S(1)} all-to-all(bf16[2,2,128,512]{3,1,0,2:T(2,128)(2,1)S(1)} %copy.66), channel_id=1, replica_groups=mesh['ctx'=128,'ch'=4] {'ctx'}, dimensions={2} | all-to-all | bytes 1048576 | tf_op jit(solution)/shard_map/all_to_all | solution.py:155
  734.6 0.8 fusion.47
  735.5 0.8 fusion.20
  736.2 0.6 reduce.1
  736.9 22.6 %all_to_all.50 = bf16[128,2,256]{2,1,0:T(2,128)(2,1)S(1)} all-to-all(bf16[128,2,256]{2,1,0:T(2,128)(2,1)S(1)} %reshape.468), channel_id=1, replica_groups=mesh['ctx'=128,'ch'=4] {'ctx'}, dimensions={0} | all-to-all | bytes 262144 | tf_op jit(solution)/shard_map/all_to_all | solution.py:160
  759.9 0.8 copy.69
  (86 shorter events, 7.7 us)
Async XLA Ops:
  7.0 20.9 %copy-start = (bf16[128,4096]{1,0:T(8,128)(2,1)S(1)}, bf16[128,4096]{1,0:T(8,128)(2,1)}, u32[]{:S(2)}) copy-start(bf16[128,4096]{1,0:T(8,128)(2,1)} %param.9) | copy-start | bytes 3145732
  7.0 566.0 %all-to-all-start = ((bf16[128,32,3,512]{3,1,2,0:T(8,128)(2,1)}), bf16[128,32,3,512]{3,1,2,0:T(8,128)(2,1)}, u32[]{:S(2)}, u32[]{:S(2)}) async-start(bf16[128,32,3,512]{3,1,2,0:T(8,128)(2,1)} %stack.17), calls=%async_computation | async-start | bytes 25165824 | tf_op jit(solution)/shard_map/all_to_all | solution.py:115
  589.7 7.7 %copy-start.1 = (f32[4096]{0:T(1024)S(1)}, f32[4096]{0:T(1024)}, u32[]{:S(2)}) copy-start(f32[4096]{0:T(1024)} %param.10) | copy-start | bytes 49156
  597.4 4.7 copy-start.2
  599.7 11.8 %collective-permute-start = (bf16[2,3,512]{0,2,1:T(8,128)(2,1)S(1)}, bf16[2,3,512]{0,2,1:T(8,128)(2,1)S(1)}, u32[]{:S(2)}, u32[]{:S(2)}) collective-permute-start(bf16[2,3,512]{0,2,1:T(8,128)(2,1)S(1)} %bitcast.133), channel_id=1, source_target_pairs={{0,4},{4,8},{8,12},{12,16},{16,20},{20,24},{24,28},{28,32},{32,36}... | collective-permute-start | bytes 18440 | tf_op jit(solution)/shard_map/ppermute | solution.py:11
  614.5 31.0 %all-to-all-start.1 = ((bf16[128,2,256]{2,1,0:T(2,128)(2,1)}), bf16[128,2,256]{2,1,0:T(2,128)(2,1)S(1)}, u32[]{:S(2)}, u32[]{:S(2)}) async-start(bf16[128,2,256]{2,1,0:T(2,128)(2,1)} %reshape.466), calls=%async_computation.1 | async-start | bytes 262144 | tf_op jit(solution)/shard_map/all_to_all | solution.py:135
  648.7 38.8 %all-to-all-start.2 = ((bf16[2,256,1,512]{3,0,2,1:T(2,128)(2,1)}), bf16[2,256,1,512]{3,0,2,1:T(2,128)(2,1)S(1)}, u32[]{:S(2)}, u32[]{:S(2)}) async-start(bf16[2,256,1,512]{3,0,2,1:T(2,128)(2,1)} %copy.60), calls=%async_computation.2 | async-start | bytes 1048576 | tf_op jit(solution)/shard_map/all_to_all | solution.py:140
  677.4 82.3 %copy-start.3 = (f32[512]{0:T(512)S(1)}, f32[512]{0:T(512)}, u32[]{:S(2)}) copy-start(f32[512]{0:T(512)} %param.15) | copy-start | bytes 6148
